TPU v7x, 256 devices: a whole 4x4x8 slice. The times are simulated.
256 devices in a mesh: seq: 16 (over x_lo, z), dp: 16 (over x_hi, y, core).
Axes of the slice: x: 4 (x_hi: 2, x_lo: 2; x = x_hi * 2 + x_lo), y: 4, z: 8, core: 2. Of those that a mesh axis runs over, the one named last changes fastest.
Arguments:
- self_query: bfloat16 [16, 2048, 2048], P('dp', 'seq'), may hold values from -13 to 13
- self_key: bfloat16 [16, 2048, 2048], P('dp', 'seq'), may hold values from -10 to 10
- self_value: bfloat16 [16, 2048, 2048], P('dp', 'seq'), may hold values from -6 to 6
- cross_query: bfloat16 [16, 2048, 2048], P('dp', 'seq'), may hold values from -6 to 6
- upstream: bfloat16 [16, 2048, 2048], P('dp', 'seq'), may hold values from -6 to 6
- caption_ids: int32 [16, 512], replicated, may hold values from 0 to 16383
- caption_lengths: int32 [16], replicated, may hold values from 64 to 512, as said below
- embed_table: bfloat16 [16384, 4096], P('dp', 'seq'), may hold values from -134 to 134
- key_weight: bfloat16 [4096, 2048], P(None, 'seq'), may hold values from -0.09375 to 0.09375
- value_weight: bfloat16 [4096, 2048], P(None, 'seq'), may hold values from -0.09375 to 0.09375
Outputs:
- grad_query: bfloat16 [16, 2048, 2048], P('dp', 'seq')
- grad_key: bfloat16 [16, 2048, 2048], P('dp', 'seq')
- grad_value: bfloat16 [16, 2048, 2048], P('dp', 'seq')
- grad_cross_query: bfloat16 [16, 2048, 2048], P('dp', 'seq')
- grad_key_weight: bfloat16 [4096, 2048], P(None, 'seq')
- grad_value_weight: bfloat16 [4096, 2048], P(None, 'seq')
Inputs may be any that keep to these rules, and one draw needn't show every extreme that they name: `caption_lengths`: some clip has exactly 512 live caption tokens and some other clip exactly 64.
All inputs are finite; a program needn't handle non-finite values.
Results may differ from a plain program's by a relative error of at most 0.024.
Values may be sent and summed in bfloat16 or wider, within the bound.
A program may use at most 128 MiB of HBM per device.

v0:
```python
import math

import jax
import jax.numpy as jnp
from jax import lax
from jax.experimental import pallas as pl
from jax.experimental.pallas import tpu as pltpu
from jax.sharding import PartitionSpec as P

MESH = pl.DeviceIdType.MESH
BF = jnp.bfloat16
F32 = jnp.float32

NZ = 8
NS = 2 * NZ
NY = 4
HD = 128
TB = 128
T = NS * TB
CAP = 512
CW = 256
HC = CW // 2
VR = 1024
BQ = 256
NQ = T // BQ
KC = 256
SCALE = HD**-0.5
LOG2 = SCALE * math.log2(math.e)


def nt(a, b):
    return lax.dot_general(a, b, (((1,), (1,)), ((), ())), preferred_element_type=F32)


def mm(a, b):
    return jnp.dot(a, b, preferred_element_type=F32)


def fold(x, op):
    return op(x.reshape(x.shape[0] // 8, 8, x.shape[1]), axis=0)


def kernel(
    sq, sk, sv, cq, up, ids, lens, table, kw, vw,
    oq, ok, ov, oc, gk, gv,
    abuf, tabt, part, relay, rsy, rsx, emb, wt, wbuf, s_ref, e_ref, l_ref, kt, acc,
    dbuf, ckv, ckt, term, wsib, wcore, wown, wfar, wstep, wrelay, wry, wxs, wrx, agw,
    a_send, a_recv, loc, t_sem, y_send, y_recv, g_send, g_recv, o_send, o_recv, w_send, w_recv,
):
    me = lax.axis_index("seq")
    my_dp = lax.axis_index("dp")
    xl, z = me // NZ, me % NZ
    core = my_dp % 2
    chip = my_dp // 2
    xh, y = chip // NY, chip % NY

    def dp_of(x_at, y_at, c_at):
        return (x_at * NY + y_at) * 2 + c_at

    y_next, y_prev, y_far = (y + 1) % NY, (y + NY - 1) % NY, (y + 2) % NY
    sib = {"dp": dp_of(xh, y, 1 - core)}
    up_y = {"dp": dp_of(xh, y_next, core)}
    down_y = {"dp": dp_of(xh, y_prev, core)}
    over_x = {"dp": dp_of(1 - xh, y, core)}
    up_z = {"seq": xl * NZ + (z + 1) % NZ}
    down_z = {"seq": xl * NZ + (z + NZ - 1) % NZ}
    over_l = {"seq": (1 - xl) * NZ + z}

    def remote(src, dst, send, recv, device):
        return pltpu.make_async_remote_copy(
            src_ref=src, dst_ref=dst, send_sem=send, recv_sem=recv, device_id=device, device_id_type=MESH
        )

    barrier = pltpu.get_barrier_semaphore()

    def greet(k, carry):
        pl.semaphore_signal(barrier, inc=1, device_id={"seq": (me + k) % NS}, device_id_type=MESH)
        return carry

    lax.fori_loop(1, NS, greet, 0)
    for other in (sib, up_y, down_y, over_x):
        pl.semaphore_signal(barrier, inc=1, device_id=other, device_id_type=MESH)
    pl.semaphore_wait(barrier, NS - 1 + 4)

    tabt[core] = table[...].T
    tab_copy = remote(tabt.at[core], tabt.at[core], t_sem.at[0], t_sem.at[1], sib)
    tab_copy.start()

    mine = pl.ds(pl.multiple_of(me * TB, TB), TB)
    sources = (sq, sk, up, sv, cq)
    for a, src in enumerate(sources):

        def send(k, carry, a=a, src=src):
            peer = (me + k) % NS
            remote(
                src.at[:, pl.ds(pl.multiple_of(peer * HD, HD), HD)],
                abuf.at[a, mine],
                a_send.at[a],
                a_recv.at[a],
                {"seq": peer},
            ).start()
            return carry

        lax.fori_loop(1, NS, send, 0)
        pltpu.make_async_copy(
            src.at[:, pl.ds(pl.multiple_of(me * HD, HD), HD)], abuf.at[a, mine], loc.at[a]
        ).start()
    w_in = [pltpu.make_async_copy(w, wbuf.at[i], loc.at[5 + i]) for i, w in enumerate((kw, vw))]
    for copy in w_in:
        copy.start()

    def arrived(a):
        most = abuf.at[a, pl.ds(0, T - TB)]
        pltpu.make_async_copy(most, most, a_recv.at[a]).wait()
        pltpu.make_async_copy(
            sources[a].at[:, pl.ds(pl.multiple_of(me * HD, HD), HD)], abuf.at[a, mine], loc.at[a]
        ).wait()

    tab_copy.wait()
    rows = lax.broadcasted_iota(jnp.int32, (KC, CAP), 0)

    def look(y_at):
        def body(x_at, carry):
            clip = dp_of(x_at, y_at, core)
            wanted = ids[pl.ds(clip, 1), :] - chip * (2 * VR)
            total = jnp.zeros((CW, CAP), F32)
            for half in range(2):
                for v in range(VR // KC):
                    hot = jnp.where(rows == wanted - (half * VR + v * KC), 1.0, 0.0).astype(BF)
                    total += mm(tabt[half, :, v * KC : (v + 1) * KC], hot)
            part[y_at, x_at] = total.astype(BF)
            return carry

        lax.fori_loop(0, 2, body, 0)

    low, high = pl.ds(0, HC), pl.ds(HC, HC)
    look(y_far)
    far_up = remote(part.at[y_far, :, high], relay.at[0], y_send.at[0], y_recv.at[0], up_y)
    far_down = remote(part.at[y_far, :, low], relay.at[1], y_send.at[1], y_recv.at[1], down_y)
    far_up.start()
    far_down.start()
    look(y_next)
    look(y_prev)
    far_up.wait_recv()
    part[y_next, :, HC:] = part[y_next, :, HC:] + relay[0]
    near_up = remote(part.at[y_next], rsy.at[0], y_send.at[2], y_recv.at[2], up_y)
    near_up.start()
    far_down.wait_recv()
    part[y_prev, :, :HC] = part[y_prev, :, :HC] + relay[1]
    near_down = remote(part.at[y_prev], rsy.at[1], y_send.at[3], y_recv.at[3], down_y)
    near_down.start()
    look(y)

    for i, copy in enumerate(w_in):
        copy.wait()
        for j in range(NS):
            wt[i * HD : (i + 1) * HD, j * CW : (j + 1) * CW] = wbuf[i, j * CW : (j + 1) * CW, :].T

    near_up.wait_recv()
    near_down.wait_recv()
    part[y, 1 - xh] = part[y, 1 - xh] + rsy[0, 1 - xh] + rsy[1, 1 - xh]
    x_copy = remote(part.at[y, 1 - xh], rsx, y_send.at[4], y_recv.at[4], over_x)
    x_copy.start()
    part[y, xh] = part[y, xh] + rsy[0, xh] + rsy[1, xh]

    def col(x_at, shift):
        return x_at * NZ + (z + shift + NZ) % NZ

    messages = {}

    def go(name, slot, part_rows, device):
        i = len(messages)
        ref = emb.at[slot] if part_rows is None else emb.at[slot, part_rows]
        messages[name] = remote(ref, ref, g_send.at[i], g_recv.at[i], device)
        messages[name].start()

    def got(name):
        messages[name].wait_recv()

    ox = 1 - xl

    def gather_start():
        x_copy.wait_recv()
        emb[me] = part[y, xh] + rsx[...]
        go("xb", me, high, over_l)
        go("p1", me, None, up_z)
        go("m1", me, None, down_z)
        go("xa", me, low, over_l)

    def gather_step(k):
        if k == 0:
            got("xb")
        else:
            got(f"pb{k}")
            got(f"mb{k}")
        if k < 3:
            go(f"pb{k + 1}", col(ox, -k), high, up_z)
            go(f"mb{k + 1}", col(ox, k), high, down_z)
        else:
            go("pb4", col(ox, -3), pl.ds(HC, HC // 2), up_z)
            go("mb4", col(ox, 3), pl.ds(HC + HC // 2, HC // 2), down_z)
        if k > 0:
            got(f"p{k}")
            got(f"m{k}")
            if k < 3:
                go(f"p{k + 1}", col(xl, -k), None, up_z)
                go(f"m{k + 1}", col(xl, k), None, down_z)
            else:
                go("p4", col(xl, -3), low, up_z)
                go("m4", col(xl, 3), high, down_z)
            go(f"fp{k}", col(xl, -k), low, over_l)
            go(f"fm{k}", col(xl, k), low, over_l)

    def gather_last():
        got("p4")
        go("f4", col(xl, 4), low, over_l)

    def gather_end():
        for name in ("xa", "pb4", "mb4", "m4", "fp1", "fm1", "fp2", "fm2", "fp3", "fm3", "f4"):
            got(name)

    def scores(queries, keys, n_keys, live):
        top = jnp.full((8, BQ), -jnp.inf, F32)
        for k in range(n_keys // KC):
            s = nt(keys[k * KC : (k + 1) * KC, :], queries)
            if live is not None:
                at = lax.broadcasted_iota(jnp.int32, (KC, BQ), 0) + k * KC
                s = jnp.where(at < live, s, -jnp.inf)
            s_ref[k * KC : (k + 1) * KC, :] = s
            top = jnp.maximum(top, fold(s, jnp.max))
        top = jnp.max(top, axis=0, keepdims=True) * LOG2
        total = jnp.zeros((8, BQ), F32)
        for k in range(n_keys // KC):
            e = jnp.exp2(s_ref[k * KC : (k + 1) * KC, :] * LOG2 - top)
            total += fold(e, jnp.sum)
            yield e.astype(BF)
        yield jnp.sum(total, axis=0, keepdims=True)

    def grads(queries, upstream, keys_t, values, n_keys, probs, total):
        inv = 1.0 / total
        delta = jnp.zeros((8, BQ), F32)
        for k in range(n_keys // KC):
            dp = nt(values[k * KC : (k + 1) * KC, :], upstream)
            s_ref[k * KC : (k + 1) * KC, :] = dp
            delta += fold(dp * probs[k * KC : (k + 1) * KC, :].astype(F32), jnp.sum)
        delta = jnp.sum(delta, axis=0, keepdims=True) * inv
        inv_rows = jnp.broadcast_to(inv, (HD, BQ)).T
        queries = (queries.astype(F32) * inv_rows).astype(BF)
        upstream = (upstream.astype(F32) * inv_rows).astype(BF)
        dq = jnp.zeros((HD, BQ), F32)
        for k in range(n_keys // KC):
            at = slice(k * KC, (k + 1) * KC)
            e = probs[at, :]
            ds = (e.astype(F32) * (s_ref[at, :] - delta)).astype(BF)
            dq += mm(keys_t[:, at], ds)
            acc[0, at, :] += mm(ds, queries)
            acc[1, at, :] += mm(e, upstream)
        return (dq * (inv * SCALE)).T.astype(BF)

    outs = (oq, ok, ov, oc)

    def post(a, peer):
        src = dbuf.at[a, pl.ds(pl.multiple_of(peer * TB, TB), TB)]
        dst = outs[a].at[:, pl.ds(pl.multiple_of(me * HD, HD), HD)]

        @pl.when(peer != me)
        def _():
            remote(src, dst, o_send.at[a], o_recv.at[a], {"seq": peer}).start()

        @pl.when(peer == me)
        def _():
            pltpu.make_async_copy(src, dst, loc.at[7 + a]).start()

    def first(q, carry):
        at = pl.ds(pl.multiple_of(q * BQ, BQ), BQ)
        for k, e in enumerate(scores(abuf[0, at, :], abuf.at[1], T, None)):
            if k < T // KC:
                e_ref[q, k * KC : (k + 1) * KC, :] = e
            else:
                l_ref[q] = e
        return carry

    def second(q, carry):
        at = pl.ds(pl.multiple_of(q * BQ, BQ), BQ)
        dbuf[0, at, :] = grads(
            abuf[0, at, :], abuf[2, at, :], kt, abuf.at[3], T, e_ref.at[q], l_ref[q]
        )
        for i in range(BQ // TB):
            post(0, q * (BQ // TB) + i)
        return carry

    arrived(0)
    arrived(1)
    for k in range(T // KC):
        kt[:, k * KC : (k + 1) * KC] = abuf[1, k * KC : (k + 1) * KC, :].T
    lax.fori_loop(0, NQ // 2, first, 0)
    gather_start()
    lax.fori_loop(NQ // 2, NQ, first, 0)
    gather_step(0)
    arrived(2)
    arrived(3)
    acc[...] = jnp.zeros_like(acc)
    lax.fori_loop(0, 2, second, 0)
    gather_step(1)
    lax.fori_loop(2, 4, second, 0)
    gather_step(2)
    lax.fori_loop(4, 6, second, 0)
    gather_step(3)
    lax.fori_loop(6, 8, second, 0)
    gather_last()

    dbuf[1] = (acc[0] * SCALE).astype(BF)
    dbuf[2] = acc[1].astype(BF)

    def post_kv(k, carry):
        peer = (me + k) % NS
        post(1, peer)
        post(2, peer)
        return carry

    lax.fori_loop(0, NS, post_kv, 0)

    gather_end()
    square = jnp.zeros((8, CAP), F32)
    kv = jnp.zeros((2 * HD, CAP), F32)
    for j in range(NS):
        block = emb[j]
        kv += mm(wt[:, j * CW : (j + 1) * CW], block)
        wide = block.astype(F32)
        square += fold(wide * wide, jnp.sum)
    mean = jnp.sum(square, axis=0, keepdims=True) * (1.0 / (NS * CW))
    rinv = lax.rsqrt(mean + 1e-06)
    kv = kv * rinv
    ckt[...] = kv[:HD, :].astype(BF)
    ckv[0] = kv[:HD, :].T.astype(BF)
    ckv[1] = kv[HD:, :].T.astype(BF)
    rinv_rows = jnp.broadcast_to(rinv, (HD, CAP)).T

    arrived(4)
    acc[:, :CAP, :] = jnp.zeros((2, CAP, HD), F32)
    live = lens[my_dp]

    def cross(q, carry):
        at = pl.ds(pl.multiple_of(q * BQ, BQ), BQ)
        queries = abuf[4, at, :]
        total = None
        for k, e in enumerate(scores(queries, ckv.at[0], CAP, live)):
            if k < CAP // KC:
                e_ref[0, k * KC : (k + 1) * KC, :] = e
            else:
                total = e
        dbuf[3, at, :] = grads(
            queries, abuf[2, at, :], ckt, ckv.at[1], CAP, e_ref.at[0], total
        )
        for i in range(BQ // TB):
            post(3, q * (BQ // TB) + i)
        return carry

    lax.fori_loop(0, NQ, cross, 0)

    term[:, :HD] = (acc[0, :CAP, :] * SCALE * rinv_rows).astype(BF)
    term[:, HD:] = (acc[1, :CAP, :] * rinv_rows).astype(BF)

    w_messages = []

    def hand(src, dst, device):
        i = len(w_messages)
        w_messages.append(remote(src, dst, w_send.at[i], w_recv.at[i], device))
        w_messages[i].start()
        return w_messages[i]

    def partial(base, out):
        def body(i, carry):
            out[i // 2, i % 2] = mm(emb[base + i], term[...]).astype(out.dtype)
            return carry

        lax.fori_loop(0, NZ, body, 0)

    partial((1 - core) * NZ, wsib)
    to_sib = hand(wsib, wcore, sib)
    partial(core * NZ, wown)
    to_sib.wait_recv()
    wown[...] = wown[...] + wcore[...].astype(F32)
    wfar[...] = wown[y_far].astype(BF)
    f_up = hand(wfar.at[:, high], wrelay.at[0], up_y)
    f_down = hand(wfar.at[:, low], wrelay.at[1], down_y)
    f_up.wait_recv()
    wstep[0, :, :HC] = wown[y_next, :, :HC].astype(BF)
    wstep[0, :, HC:] = (wown[y_next, :, HC:] + wrelay[0].astype(F32)).astype(BF)
    n_up = hand(wstep.at[0], wry.at[0], up_y)
    f_down.wait_recv()
    wstep[1, :, :HC] = (wown[y_prev, :, :HC] + wrelay[1].astype(F32)).astype(BF)
    wstep[1, :, HC:] = wown[y_prev, :, HC:].astype(BF)
    n_down = hand(wstep.at[1], wry.at[1], down_y)
    n_up.wait_recv()
    n_down.wait_recv()

    def here(x_at):
        return wown[y, x_at] + wry[0, x_at].astype(F32) + wry[1, x_at].astype(F32)

    wxs[...] = here(1 - xh).astype(BF)
    x_half = hand(wxs, wrx, over_x)
    mine_sum = here(xh)
    x_half.wait_recv()
    agw[core, y, xh] = (mine_sum + wrx[...].astype(F32)).astype(BF)
    own = agw.at[core, y, xh]
    x_back = hand(own, own, over_x)
    x_back.wait_recv()
    row = agw.at[core, y]
    b_up = hand(row, row, up_y)
    b_down = hand(row, row, down_y)
    backs = [hand(row, row, sib)]
    b_up.wait_recv()
    upper = agw.at[core, y_prev, :, high]
    c_up = hand(upper, upper, up_y)
    b_down.wait_recv()
    lower = agw.at[core, y_next, :, low]
    c_down = hand(lower, lower, down_y)
    for at in (y_prev, y_next):
        backs.append(hand(agw.at[core, at], agw.at[core, at], sib))
    c_up.wait_recv()
    c_down.wait_recv()
    backs.append(hand(agw.at[core, y_far], agw.at[core, y_far], sib))
    for message in backs:
        message.wait_recv()
    leave = [
        pltpu.make_async_copy(agw.at[:, :, :, :, i * HD : (i + 1) * HD], dst, loc.at[11 + i])
        for i, dst in enumerate((gk, gv))
    ]
    for copy in leave:
        copy.start()

    for copy in leave:
        copy.wait()
    tabless = (far_up, far_down, near_up, near_down, x_copy)
    for message in (*tabless, *messages.values(), *w_messages):
        message.wait_send()
    most = abuf.at[0, pl.ds(0, T - TB)]
    for a in range(5):
        pltpu.make_async_copy(most, most, a_send.at[a]).wait()
    for a in range(4):
        pltpu.make_async_copy(most, most, o_send.at[a]).wait()
        pltpu.make_async_copy(most, most, o_recv.at[a]).wait()
        src = dbuf.at[a, pl.ds(pl.multiple_of(me * TB, TB), TB)]
        dst = outs[a].at[:, pl.ds(pl.multiple_of(me * HD, HD), HD)]
        pltpu.make_async_copy(src, dst, loc.at[7 + a]).wait()


def on_device(
    self_query,
    self_key,
    self_value,
    cross_query,
    upstream,
    caption_ids,
    caption_lengths,
    embed_table,
    key_weight,
    value_weight,
):
    tokens = [x[0] for x in (self_query, self_key, self_value, cross_query, upstream)]
    anywhere = pl.BlockSpec(memory_space=pl.ANY)
    vmem = pl.BlockSpec(memory_space=pltpu.VMEM)
    smem = pl.BlockSpec(memory_space=pltpu.SMEM)
    token_grad = jax.ShapeDtypeStruct((TB, NS * HD), BF)
    weight_grad = jax.ShapeDtypeStruct((2, NY, 2, CW, HD), BF)
    n_gather = 25
    n_sum = 15
    dma = pltpu.SemaphoreType.DMA
    results = pl.pallas_call(
        kernel,
        out_shape=[token_grad] * 4 + [weight_grad] * 2,
        in_specs=[anywhere] * 5 + [vmem, smem, vmem, anywhere, anywhere],
        out_specs=[anywhere] * 6,
        scratch_shapes=[
            pltpu.VMEM((5, T, HD), BF),
            pltpu.VMEM((2, CW, VR), BF),
            pltpu.VMEM((NY, 2, CW, CAP), BF),
            pltpu.VMEM((2, 2, HC, CAP), BF),
            pltpu.VMEM((2, 2, CW, CAP), BF),
            pltpu.VMEM((CW, CAP), BF),
            pltpu.VMEM((NS, CW, CAP), BF),
            pltpu.VMEM((2 * HD, NS * CW), BF),
            pltpu.VMEM((2, NS * CW, HD), BF),
            pltpu.VMEM((T, BQ), F32),
            pltpu.VMEM((NQ, T, BQ), BF),
            pltpu.VMEM((NQ, 1, BQ), F32),
            pltpu.VMEM((HD, T), BF),
            pltpu.VMEM((2, T, HD), F32),
            pltpu.VMEM((4, T, HD), BF),
            pltpu.VMEM((2, CAP, HD), BF),
            pltpu.VMEM((HD, CAP), BF),
            pltpu.VMEM((CAP, 2 * HD), BF),
            pltpu.VMEM((NY, 2, CW, 2 * HD), BF),
            pltpu.VMEM((NY, 2, CW, 2 * HD), BF),
            pltpu.VMEM((NY, 2, CW, 2 * HD), F32),
            pltpu.VMEM((2, CW, 2 * HD), BF),
            pltpu.VMEM((2, 2, CW, 2 * HD), BF),
            pltpu.VMEM((2, 2, HC, 2 * HD), BF),
            pltpu.VMEM((2, 2, CW, 2 * HD), BF),
            pltpu.VMEM((CW, 2 * HD), BF),
            pltpu.VMEM((CW, 2 * HD), BF),
            pltpu.VMEM((2, NY, 2, CW, 2 * HD), BF),
            dma((5,)),
            dma((5,)),
            dma((13,)),
            dma((2,)),
            dma((5,)),
            dma((5,)),
            dma((n_gather,)),
            dma((n_gather,)),
            dma((4,)),
            dma((4,)),
            dma((n_sum,)),
            dma((n_sum,)),
        ],
        compiler_params=pltpu.CompilerParams(
            collective_id=0, has_side_effects=True, vmem_limit_bytes=56 * 1024 * 1024
        ),
    )(*tokens, caption_ids, caption_lengths, embed_table, key_weight, value_weight)
    rows = NS * CW
    return tuple(r[None] for r in results[:4]) + tuple(r.reshape(rows, HD) for r in results[4:])


def solution(mesh):
    placed = (
        P("dp", "seq", None),
        P("dp", "seq", None),
        P("dp", "seq", None),
        P("dp", "seq", None),
        P("dp", "seq", None),
        P(),
        P(),
        P("dp", "seq"),
        P(None, "seq"),
        P(None, "seq"),
    )
    return jax.shard_map(
        on_device,
        mesh=mesh,
        in_specs=placed,
        out_specs=(
            P("dp", "seq", None),
            P("dp", "seq", None),
            P("dp", "seq", None),
            P("dp", "seq", None),
            P(None, "seq"),
            P(None, "seq"),
        ),
        check_vma=False,
    )
```

profile of v0, /device:TPU:1, one launch (start us, length us, event | category | flops | bytes accessed | tf_op | source)
XLA Modules:
  0.0 180.9 jit_solution(5808786074072828150)
XLA Ops:
  0.6 172.9 %shard_map.145 = (bf16[128,2048]{1,0:T(8,128)(2,1)}, bf16[128,2048]{1,0:T(8,128)(2,1)}, bf16[128,2048]{1,0:T(8,128)(2,1)}, bf16[128,2048]{1,0:T(8,128)(2,1)}, bf...) custom-call(bf16[128,2048]{1,0:T(8,128)(2,1)} %bitcast.17, bf16[128,2048]{1,0:T(8,128)(2,1)} %bitcast.18, ...), custom_call_target="tpu_custom_call" | custom-call | tf_op jit(solution)/shard_map/pallas_call | solution.py:470
  173.6 0.0 copy-start.4
  173.6 1.9 %copy.22 = bf16[1,128,2048]{2,1,0:T(8,128)(2,1)} copy(bf16[1,128,2048]{2,1,0:T(8,128)(2,1)} %bitcast.16) | data formatting | bytes 1048576
  175.5 0.0 copy-done.4
  175.5 0.0 copy-start.3
  175.5 0.0 copy-start.2
  175.5 0.8 copy.23
  176.3 0.4 copy-done.3
  176.8 0.0 copy-start.1
  176.8 0.8 copy.24
  177.6 0.0 copy-done.2
  177.6 0.8 copy.25
  178.4 0.0 copy-done.1
  178.4 0.0 copy-start
  178.4 1.0 copy.26
  179.3 0.6 copy-done
  180.0 1.0 copy.27
Async XLA Ops:
  173.6 2.0 %copy-start.4 = (bf16[128,2048]{1,0:T(8,128)(2,1)S(1)}, bf16[128,2048]{1,0:T(8,128)(2,1)}, u32[]{:S(2)}) copy-start(bf16[128,2048]{1,0:T(8,128)(2,1)} %get-tuple-element.13) | copy-start | bytes 1572868
  175.5 1.2 copy-start.3
  175.5 2.0 %copy-start.2 = (bf16[128,2048]{1,0:T(8,128)(2,1)S(1)}, bf16[128,2048]{1,0:T(8,128)(2,1)}, u32[]{:S(2)}) copy-start(bf16[128,2048]{1,0:T(8,128)(2,1)} %get-tuple-element.15) | copy-start | bytes 1572868
  176.8 1.6 copy-start.1
  178.4 1.6 copy-start
where the time goes:
time: 182 us; the launch traced here: 181 us
  Pallas kernels  173 us (95%)
  local copies, waits for them, and re-layouts  7.34 us (4%)
    pallas_call x1, Pallas kernels, on_device(): pl.pallas_call(kernel, out_shape=[token_grad] * 4 + [weight_grad] * 2, in...  173 us
    unnamed x16, local copies, waits for them, and re-layouts  7.34 us

commit v1 on v0

--- a/solution.py
+++ b/solution.py
@@ -25,6 +25,8 @@
 NQ = T // BQ
 KC = 256
 SCALE = HD**-0.5
+EARLY = (0, 1, 2)
+AFTER = {"step1": (4,), "step3": (3,)}
 LOG2 = SCALE * math.log2(math.e)
 
 
@@ -42,10 +44,10 @@
 
 def kernel(
     sq, sk, sv, cq, up, ids, lens, table, kw, vw,
-    oq, ok, ov, oc, gk, gv,
-    abuf, tabt, part, relay, rsy, rsx, emb, wt, wbuf, s_ref, e_ref, l_ref, kt, acc,
+    oq, ok, ov, oc, gw,
+    abuf, tabt, part, relay, rsy, emb, wt, wbuf, s_ref, e_ref, ec_ref, l_ref, kt, acc,
     dbuf, ckv, ckt, term, wsib, wcore, wown, wfar, wstep, wrelay, wry, wxs, wrx, agw,
-    a_send, a_recv, loc, t_sem, y_send, y_recv, g_send, g_recv, o_send, o_recv, w_send, w_recv,
+    a_send, a_recv, loc, t_send, t_recv, y_send, y_recv, g_send, g_recv, o_send, o_recv, w_send, w_recv,
 ):
     me = lax.axis_index("seq")
     my_dp = lax.axis_index("dp")
@@ -82,16 +84,21 @@
         pl.semaphore_signal(barrier, inc=1, device_id=other, device_id_type=MESH)
     pl.semaphore_wait(barrier, NS - 1 + 4)
 
-    tabt[core] = table[...].T
-    tab_copy = remote(tabt.at[core], tabt.at[core], t_sem.at[0], t_sem.at[1], sib)
-    tab_copy.start()
+    tabt[0, core] = table[...].T
+    table_over = remote(tabt.at[0, core], tabt.at[1, core], t_send.at[0], t_recv.at[0], over_x)
+    table_over.start()
+    table_sib = remote(tabt.at[0, core], tabt.at[0, core], t_send.at[1], t_recv.at[1], sib)
+    table_sib.start()
 
     mine = pl.ds(pl.multiple_of(me * TB, TB), TB)
     sources = (sq, sk, up, sv, cq)
-    for a, src in enumerate(sources):
-
-        def send(k, carry, a=a, src=src):
-            peer = (me + k) % NS
+
+    def send_in(a, dx):
+        src = sources[a]
+
+        def send(step, carry):
+            dz = (step + 1) // 2 * (2 * (step % 2) - 1)
+            peer = (xl + dx) % 2 * NZ + (z + dz + NZ) % NZ
             remote(
                 src.at[:, pl.ds(pl.multiple_of(peer * HD, HD), HD)],
                 abuf.at[a, mine],
@@ -101,10 +108,15 @@
             ).start()
             return carry
 
-        lax.fori_loop(1, NS, send, 0)
+        lax.fori_loop(1 - dx, NZ, send, 0)
+
+    for a in (0, 1, 2, 4, 3):
         pltpu.make_async_copy(
-            src.at[:, pl.ds(pl.multiple_of(me * HD, HD), HD)], abuf.at[a, mine], loc.at[a]
+            sources[a].at[:, pl.ds(pl.multiple_of(me * HD, HD), HD)], abuf.at[a, mine], loc.at[a]
         ).start()
+    for dx in range(2):
+        for a in EARLY:
+            send_in(a, dx)
     w_in = [pltpu.make_async_copy(w, wbuf.at[i], loc.at[5 + i]) for i, w in enumerate((kw, vw))]
     for copy in w_in:
         copy.start()
@@ -116,52 +128,58 @@
             sources[a].at[:, pl.ds(pl.multiple_of(me * HD, HD), HD)], abuf.at[a, mine], loc.at[a]
         ).wait()
 
-    tab_copy.wait()
     rows = lax.broadcasted_iota(jnp.int32, (KC, CAP), 0)
 
-    def look(y_at):
-        def body(x_at, carry):
-            clip = dp_of(x_at, y_at, core)
-            wanted = ids[pl.ds(clip, 1), :] - chip * (2 * VR)
-            total = jnp.zeros((CW, CAP), F32)
-            for half in range(2):
-                for v in range(VR // KC):
-                    hot = jnp.where(rows == wanted - (half * VR + v * KC), 1.0, 0.0).astype(BF)
-                    total += mm(tabt[half, :, v * KC : (v + 1) * KC], hot)
-            part[y_at, x_at] = total.astype(BF)
-            return carry
-
-        lax.fori_loop(0, 2, body, 0)
-
-    low, high = pl.ds(0, HC), pl.ds(HC, HC)
-    look(y_far)
-    far_up = remote(part.at[y_far, :, high], relay.at[0], y_send.at[0], y_recv.at[0], up_y)
-    far_down = remote(part.at[y_far, :, low], relay.at[1], y_send.at[1], y_recv.at[1], down_y)
-    far_up.start()
-    far_down.start()
-    look(y_next)
-    look(y_prev)
-    far_up.wait_recv()
-    part[y_next, :, HC:] = part[y_next, :, HC:] + relay[0]
-    near_up = remote(part.at[y_next], rsy.at[0], y_send.at[2], y_recv.at[2], up_y)
-    near_up.start()
-    far_down.wait_recv()
-    part[y_prev, :, :HC] = part[y_prev, :, :HC] + relay[1]
-    near_down = remote(part.at[y_prev], rsy.at[1], y_send.at[3], y_recv.at[3], down_y)
-    near_down.start()
-    look(y)
+    def look(i, x_at, y_at):
+        wanted = ids[pl.ds(dp_of(xh, y_at, core), 1), :] - dp_of(x_at, y, 0) * VR
+        total = jnp.zeros((CW, CAP), F32)
+        for half in range(2):
+            for v in range(VR // KC):
+                hot = jnp.where(rows == wanted - (half * VR + v * KC), 1.0, 0.0).astype(BF)
+                total += mm(tabt[i, half, :, v * KC : (v + 1) * KC], hot)
+        return total.astype(BF)
+
+    def look_here(k, carry):
+        y_at = (y + k) % NY
+        part[y_at] = look(0, xh, y_at)
+        return carry
+
+    def look_there(k, carry):
+        y_at = (y + k) % NY
+        part[y_at] = part[y_at] + look(1, 1 - xh, y_at)
+        return carry
+
+    table_sib.wait_recv()
+    lax.fori_loop(0, NY, look_here, 0)
+    table_over.wait_recv()
+    table_on = remote(tabt.at[1, core], tabt.at[1, core], t_send.at[2], t_recv.at[2], sib)
+    table_on.start()
 
     for i, copy in enumerate(w_in):
         copy.wait()
         for j in range(NS):
             wt[i * HD : (i + 1) * HD, j * CW : (j + 1) * CW] = wbuf[i, j * CW : (j + 1) * CW, :].T
 
+    low, high = pl.ds(0, HC), pl.ds(HC, HC)
+    table_on.wait_recv()
+    look_there(2, 0)
+    far_up = remote(part.at[y_far, high], relay.at[0], y_send.at[0], y_recv.at[0], up_y)
+    far_down = remote(part.at[y_far, low], relay.at[1], y_send.at[1], y_recv.at[1], down_y)
+    far_up.start()
+    far_down.start()
+    look_there(1, 0)
+    far_up.wait_recv()
+    part[y_next, HC:] = part[y_next, HC:] + relay[0]
+    near_up = remote(part.at[y_next], rsy.at[0], y_send.at[2], y_recv.at[2], up_y)
+    near_up.start()
+    look_there(3, 0)
+    far_down.wait_recv()
+    part[y_prev, :HC] = part[y_prev, :HC] + relay[1]
+    near_down = remote(part.at[y_prev], rsy.at[1], y_send.at[3], y_recv.at[3], down_y)
+    near_down.start()
+    look_there(0, 0)
     near_up.wait_recv()
     near_down.wait_recv()
-    part[y, 1 - xh] = part[y, 1 - xh] + rsy[0, 1 - xh] + rsy[1, 1 - xh]
-    x_copy = remote(part.at[y, 1 - xh], rsx, y_send.at[4], y_recv.at[4], over_x)
-    x_copy.start()
-    part[y, xh] = part[y, xh] + rsy[0, xh] + rsy[1, xh]
 
     def col(x_at, shift):
         return x_at * NZ + (z + shift + NZ) % NZ
@@ -180,43 +198,45 @@
     ox = 1 - xl
 
     def gather_start():
-        x_copy.wait_recv()
-        emb[me] = part[y, xh] + rsx[...]
+        emb[me] = part[y] + rsy[0] + rsy[1]
+        go("pl1", me, low, up_z)
+        go("ml1", me, low, down_z)
         go("xb", me, high, over_l)
-        go("p1", me, None, up_z)
-        go("m1", me, None, down_z)
+        go("ph1", me, high, up_z)
+        go("mh1", me, high, down_z)
         go("xa", me, low, over_l)
 
     def gather_step(k):
-        if k == 0:
-            got("xb")
-        else:
+        if k > 0:
+            got(f"pl{k}")
+            got(f"ml{k}")
+            go(f"pl{k + 1}", col(xl, -k), low, up_z)
+            if k < 3:
+                go(f"ml{k + 1}", col(xl, k), low, down_z)
+            go(f"fp{k}", col(xl, -k), low, over_l)
+            go(f"fm{k}", col(xl, k), low, over_l)
+            got(f"ph{k}")
+            got(f"mh{k}")
+            if k < 3:
+                go(f"ph{k + 1}", col(xl, -k), high, up_z)
+            go(f"mh{k + 1}", col(xl, k), high, down_z)
             got(f"pb{k}")
             got(f"mb{k}")
+        else:
+            got("xb")
         if k < 3:
             go(f"pb{k + 1}", col(ox, -k), high, up_z)
             go(f"mb{k + 1}", col(ox, k), high, down_z)
         else:
             go("pb4", col(ox, -3), pl.ds(HC, HC // 2), up_z)
             go("mb4", col(ox, 3), pl.ds(HC + HC // 2, HC // 2), down_z)
-        if k > 0:
-            got(f"p{k}")
-            got(f"m{k}")
-            if k < 3:
-                go(f"p{k + 1}", col(xl, -k), None, up_z)
-                go(f"m{k + 1}", col(xl, k), None, down_z)
-            else:
-                go("p4", col(xl, -3), low, up_z)
-                go("m4", col(xl, 3), high, down_z)
-            go(f"fp{k}", col(xl, -k), low, over_l)
-            go(f"fm{k}", col(xl, k), low, over_l)
 
     def gather_last():
-        got("p4")
+        got("pl4")
         go("f4", col(xl, 4), low, over_l)
 
     def gather_end():
-        for name in ("xa", "pb4", "mb4", "m4", "fp1", "fm1", "fp2", "fm2", "fp3", "fm3", "f4"):
+        for name in ("mh4", "xa", "pb4", "mb4", "fp1", "fm1", "fp2", "fm2", "fp3", "fm3", "f4"):
             got(name)
 
     def scores(queries, keys, n_keys, live):
@@ -289,36 +309,30 @@
             post(0, q * (BQ // TB) + i)
         return carry
 
+    def later(point):
+        for a in AFTER.get(point, ()):
+            for dx in range(2):
+                send_in(a, dx)
+
+    gather_start()
+    later("start")
     arrived(0)
     arrived(1)
     for k in range(T // KC):
         kt[:, k * KC : (k + 1) * KC] = abuf[1, k * KC : (k + 1) * KC, :].T
-    lax.fori_loop(0, NQ // 2, first, 0)
-    gather_start()
-    lax.fori_loop(NQ // 2, NQ, first, 0)
+    lax.fori_loop(0, 2, first, 0)
     gather_step(0)
-    arrived(2)
-    arrived(3)
-    acc[...] = jnp.zeros_like(acc)
-    lax.fori_loop(0, 2, second, 0)
+    later("step0")
+    lax.fori_loop(2, 4, first, 0)
     gather_step(1)
-    lax.fori_loop(2, 4, second, 0)
+    later("step1")
+    lax.fori_loop(4, 6, first, 0)
     gather_step(2)
-    lax.fori_loop(4, 6, second, 0)
+    later("step2")
+    lax.fori_loop(6, 8, first, 0)
     gather_step(3)
-    lax.fori_loop(6, 8, second, 0)
+    later("step3")
     gather_last()
-
-    dbuf[1] = (acc[0] * SCALE).astype(BF)
-    dbuf[2] = acc[1].astype(BF)
-
-    def post_kv(k, carry):
-        peer = (me + k) % NS
-        post(1, peer)
-        post(2, peer)
-        return carry
-
-    lax.fori_loop(0, NS, post_kv, 0)
 
     gather_end()
     square = jnp.zeros((8, CAP), F32)
@@ -336,6 +350,7 @@
     ckv[1] = kv[HD:, :].T.astype(BF)
     rinv_rows = jnp.broadcast_to(rinv, (HD, CAP)).T
 
+    arrived(2)
     arrived(4)
     acc[:, :CAP, :] = jnp.zeros((2, CAP, HD), F32)
     live = lens[my_dp]
@@ -346,11 +361,11 @@
         total = None
         for k, e in enumerate(scores(queries, ckv.at[0], CAP, live)):
             if k < CAP // KC:
-                e_ref[0, k * KC : (k + 1) * KC, :] = e
+                ec_ref[k * KC : (k + 1) * KC, :] = e
             else:
                 total = e
         dbuf[3, at, :] = grads(
-            queries, abuf[2, at, :], ckt, ckv.at[1], CAP, e_ref.at[0], total
+            queries, abuf[2, at, :], ckt, ckv.at[1], CAP, ec_ref, total
         )
         for i in range(BQ // TB):
             post(3, q * (BQ // TB) + i)
@@ -376,64 +391,108 @@
 
         lax.fori_loop(0, NZ, body, 0)
 
+    def reduction(p):
+        at = pl.ds(p * HD, HD)
+        to_sib = hand(wsib.at[:, :, :, at], wcore.at[:, :, :, at], sib)
+        if p == 0:
+            partial(core * NZ, wown)
+        yield
+        to_sib.wait_recv()
+        wfar[:, :, at] = (wown[y_far, :, :, at] + wcore[y_far, :, :, at].astype(F32)).astype(BF)
+        f_up = hand(wfar.at[:, high, at], wrelay.at[0, :, :, at], up_y)
+        f_down = hand(wfar.at[:, low, at], wrelay.at[1, :, :, at], down_y)
+        for slot in (y_next, y_prev, y):
+            wown[slot, :, :, at] = wown[slot, :, :, at] + wcore[slot, :, :, at].astype(F32)
+        yield
+        f_up.wait_recv()
+        wstep[0, :, low, at] = wown[y_next, :, low, at].astype(BF)
+        wstep[0, :, high, at] = (wown[y_next, :, high, at] + wrelay[0, :, :, at].astype(F32)).astype(BF)
+        n_up = hand(wstep.at[0, :, :, at], wry.at[0, :, :, at], up_y)
+        f_down.wait_recv()
+        wstep[1, :, low, at] = (wown[y_prev, :, low, at] + wrelay[1, :, :, at].astype(F32)).astype(BF)
+        wstep[1, :, high, at] = wown[y_prev, :, high, at].astype(BF)
+        n_down = hand(wstep.at[1, :, :, at], wry.at[1, :, :, at], down_y)
+        yield
+        n_up.wait_recv()
+        n_down.wait_recv()
+
+        def here(x_at):
+            return (
+                wown[y, x_at, :, at]
+                + wry[0, x_at, :, at].astype(F32)
+                + wry[1, x_at, :, at].astype(F32)
+            )
+
+        wxs[:, at] = here(1 - xh).astype(BF)
+        x_half = hand(wxs.at[:, at], wrx.at[:, at], over_x)
+        mine_sum = here(xh)
+        yield
+        x_half.wait_recv()
+        agw[core, y, xh, :, at] = (mine_sum + wrx[:, at].astype(F32)).astype(BF)
+        own = agw.at[core, y, xh, :, at]
+        x_back = hand(own, own, over_x)
+        yield
+        x_back.wait_recv()
+        row = agw.at[core, y, :, :, at]
+        b_up = hand(row, row, up_y)
+        b_down = hand(row, row, down_y)
+        backs = [hand(row, row, sib)]
+        yield
+        b_up.wait_recv()
+        upper = agw.at[core, y_prev, :, high, at]
+        c_up = hand(upper, upper, up_y)
+        b_down.wait_recv()
+        lower = agw.at[core, y_next, :, low, at]
+        c_down = hand(lower, lower, down_y)
+        for slot in (y_prev, y_next):
+            block = agw.at[core, slot, :, :, at]
+            backs.append(hand(block, block, sib))
+        yield
+        c_up.wait_recv()
+        c_down.wait_recv()
+        block = agw.at[core, y_far, :, :, at]
+        backs.append(hand(block, block, sib))
+        yield
+        for message in backs:
+            message.wait_recv()
+        yield
+
     partial((1 - core) * NZ, wsib)
-    to_sib = hand(wsib, wcore, sib)
-    partial(core * NZ, wown)
-    to_sib.wait_recv()
-    wown[...] = wown[...] + wcore[...].astype(F32)
-    wfar[...] = wown[y_far].astype(BF)
-    f_up = hand(wfar.at[:, high], wrelay.at[0], up_y)
-    f_down = hand(wfar.at[:, low], wrelay.at[1], down_y)
-    f_up.wait_recv()
-    wstep[0, :, :HC] = wown[y_next, :, :HC].astype(BF)
-    wstep[0, :, HC:] = (wown[y_next, :, HC:] + wrelay[0].astype(F32)).astype(BF)
-    n_up = hand(wstep.at[0], wry.at[0], up_y)
-    f_down.wait_recv()
-    wstep[1, :, :HC] = (wown[y_prev, :, :HC] + wrelay[1].astype(F32)).astype(BF)
-    wstep[1, :, HC:] = wown[y_prev, :, HC:].astype(BF)
-    n_down = hand(wstep.at[1], wry.at[1], down_y)
-    n_up.wait_recv()
-    n_down.wait_recv()
-
-    def here(x_at):
-        return wown[y, x_at] + wry[0, x_at].astype(F32) + wry[1, x_at].astype(F32)
-
-    wxs[...] = here(1 - xh).astype(BF)
-    x_half = hand(wxs, wrx, over_x)
-    mine_sum = here(xh)
-    x_half.wait_recv()
-    agw[core, y, xh] = (mine_sum + wrx[...].astype(F32)).astype(BF)
-    own = agw.at[core, y, xh]
-    x_back = hand(own, own, over_x)
-    x_back.wait_recv()
-    row = agw.at[core, y]
-    b_up = hand(row, row, up_y)
-    b_down = hand(row, row, down_y)
-    backs = [hand(row, row, sib)]
-    b_up.wait_recv()
-    upper = agw.at[core, y_prev, :, high]
-    c_up = hand(upper, upper, up_y)
-    b_down.wait_recv()
-    lower = agw.at[core, y_next, :, low]
-    c_down = hand(lower, lower, down_y)
-    for at in (y_prev, y_next):
-        backs.append(hand(agw.at[core, at], agw.at[core, at], sib))
-    c_up.wait_recv()
-    c_down.wait_recv()
-    backs.append(hand(agw.at[core, y_far], agw.at[core, y_far], sib))
-    for message in backs:
-        message.wait_recv()
-    leave = [
-        pltpu.make_async_copy(agw.at[:, :, :, :, i * HD : (i + 1) * HD], dst, loc.at[11 + i])
-        for i, dst in enumerate((gk, gv))
-    ]
+    sums = [reduction(0), reduction(1)]
+
+    def stage():
+        for part_sum in sums:
+            next(part_sum)
+
+    stage()
+    arrived(3)
+    acc[...] = jnp.zeros_like(acc)
+    lax.fori_loop(0, 2, second, 0)
+    stage()
+    lax.fori_loop(2, 5, second, 0)
+    stage()
+    lax.fori_loop(5, 8, second, 0)
+    dbuf[1] = (acc[0] * SCALE).astype(BF)
+    dbuf[2] = acc[1].astype(BF)
+
+    def post_kv(k, carry):
+        peer = (me + k) % NS
+        post(1, peer)
+        post(2, peer)
+        return carry
+
+    lax.fori_loop(0, NS, post_kv, 0)
+    for _ in range(6):
+        stage()
+    leave = [pltpu.make_async_copy(agw, gw, loc.at[11])]
     for copy in leave:
         copy.start()
 
     for copy in leave:
         copy.wait()
-    tabless = (far_up, far_down, near_up, near_down, x_copy)
-    for message in (*tabless, *messages.values(), *w_messages):
+    tables = (table_over, table_sib, table_on)
+    parts = (far_up, far_down, near_up, near_down)
+    for message in (*tables, *parts, *messages.values(), *w_messages):
         message.wait_send()
     most = abuf.at[0, pl.ds(0, T - TB)]
     for a in range(5):
@@ -444,6 +503,13 @@
         src = dbuf.at[a, pl.ds(pl.multiple_of(me * TB, TB), TB)]
         dst = outs[a].at[:, pl.ds(pl.multiple_of(me * HD, HD), HD)]
         pltpu.make_async_copy(src, dst, loc.at[7 + a]).wait()
+
+
+def leave_kernel(q, k, v, c, w, oq, ok, ov, oc, gk, gv):
+    for src, dst in ((q, oq), (k, ok), (v, ov), (c, oc)):
+        dst[0] = src[...]
+    gk[...] = w[:, :HD]
+    gv[...] = w[:, HD:]
 
 
 def on_device(
@@ -463,27 +529,27 @@
     vmem = pl.BlockSpec(memory_space=pltpu.VMEM)
     smem = pl.BlockSpec(memory_space=pltpu.SMEM)
     token_grad = jax.ShapeDtypeStruct((TB, NS * HD), BF)
-    weight_grad = jax.ShapeDtypeStruct((2, NY, 2, CW, HD), BF)
-    n_gather = 25
-    n_sum = 15
+    weight_grads = jax.ShapeDtypeStruct((2, NY, 2, CW, 2 * HD), BF)
+    n_gather = 31
+    n_sum = 30
     dma = pltpu.SemaphoreType.DMA
     results = pl.pallas_call(
         kernel,
-        out_shape=[token_grad] * 4 + [weight_grad] * 2,
+        out_shape=[token_grad] * 4 + [weight_grads],
         in_specs=[anywhere] * 5 + [vmem, smem, vmem, anywhere, anywhere],
-        out_specs=[anywhere] * 6,
+        out_specs=[anywhere] * 5,
         scratch_shapes=[
             pltpu.VMEM((5, T, HD), BF),
-            pltpu.VMEM((2, CW, VR), BF),
-            pltpu.VMEM((NY, 2, CW, CAP), BF),
-            pltpu.VMEM((2, 2, HC, CAP), BF),
-            pltpu.VMEM((2, 2, CW, CAP), BF),
-            pltpu.VMEM((CW, CAP), BF),
+            pltpu.VMEM((2, 2, CW, VR), BF),
+            pltpu.VMEM((NY, CW, CAP), BF),
+            pltpu.VMEM((2, HC, CAP), BF),
+            pltpu.VMEM((2, CW, CAP), BF),
             pltpu.VMEM((NS, CW, CAP), BF),
             pltpu.VMEM((2 * HD, NS * CW), BF),
             pltpu.VMEM((2, NS * CW, HD), BF),
             pltpu.VMEM((T, BQ), F32),
             pltpu.VMEM((NQ, T, BQ), BF),
+            pltpu.VMEM((CAP, BQ), BF),
             pltpu.VMEM((NQ, 1, BQ), F32),
             pltpu.VMEM((HD, T), BF),
             pltpu.VMEM((2, T, HD), F32),
@@ -503,10 +569,11 @@
             pltpu.VMEM((2, NY, 2, CW, 2 * HD), BF),
             dma((5,)),
             dma((5,)),
-            dma((13,)),
-            dma((2,)),
-            dma((5,)),
-            dma((5,)),
+            dma((12,)),
+            dma((3,)),
+            dma((3,)),
+            dma((4,)),
+            dma((4,)),
             dma((n_gather,)),
             dma((n_gather,)),
             dma((4,)),
@@ -519,7 +586,17 @@
         ),
     )(*tokens, caption_ids, caption_lengths, embed_table, key_weight, value_weight)
     rows = NS * CW
-    return tuple(r[None] for r in results[:4]) + tuple(r.reshape(rows, HD) for r in results[4:])
+    cuts = 4
+    token_in = pl.BlockSpec((TB // cuts, NS * HD), lambda i: (i, 0))
+    token_out = pl.BlockSpec((1, TB // cuts, NS * HD), lambda i: (0, i, 0))
+    return pl.pallas_call(
+        leave_kernel,
+        grid=(cuts,),
+        out_shape=[jax.ShapeDtypeStruct((1, TB, NS * HD), BF)] * 4
+        + [jax.ShapeDtypeStruct((rows, HD), BF)] * 2,
+        in_specs=[token_in] * 4 + [pl.BlockSpec((rows // cuts, 2 * HD), lambda i: (i, 0))],
+        out_specs=[token_out] * 4 + [pl.BlockSpec((rows // cuts, HD), lambda i: (i, 0))] * 2,
+    )(*results[:4], results[4].reshape(rows, 2 * HD))
 
 
 def solution(mesh):

time: 182 us -> 158 us (0.87)
  Pallas kernels: 173 us -> 157 us
  local copies, waits for them, and re-layouts: 7.34 us -> 0 us
    pallas_call x1 -> x2, Pallas kernels: 173 us -> 157 us  [the longest x1 152 us: on_device(): pl.pallas_call(kernel, out_shape=[token_grad] * 4 + [weight_grads], in_sp...]
    unnamed x16 -> x0, local copies, waits for them, and re-layouts: 7.34 us -> none
where the time goes in v1:
time: 158 us; the launch traced here: 157 us
  Pallas kernels  157 us (99%)
    pallas_call x1, Pallas kernels, on_device(): pl.pallas_call(kernel, out_shape=[token_grad] * 4 + [weight_grads], in_sp...  152 us
    pallas_call x1, Pallas kernels, on_device(): pl.pallas_call(leave_kernel, grid=(cuts,), out_shape=[jax.ShapeDtypeStruc...  4.89 us

profile of v1, /device:TPU:1, one launch (start us, length us, event | category | flops | bytes accessed | tf_op | source)
XLA Modules:
  0.0 157.3 jit_solution(3128007490913589456)
XLA Ops:
  0.6 151.7 %shard_map.145 = (bf16[128,2048]{1,0:T(8,128)(2,1)}, bf16[128,2048]{1,0:T(8,128)(2,1)}, bf16[128,2048]{1,0:T(8,128)(2,1)}, bf16[128,2048]{1,0:T(8,128)(2,1)}, bf16[2,4,2,256,256]{4,3,2,1,0:T(8,128)(2,1)}) custom-call(bf16[128,2048]{1,0:T(8,128)(2,1)} %bitcast.7, bf16[128,2048]{1,0:T(8,128)(2,1)} %bitcast.8, bf16[128,2048]{1,0:T(8,128)(2,1)} %bitcast.9, ...), custom_call_target="tpu_custom_call" | custom-call | tf_op jit(solution)/shard_map/pallas_call | solution.py:536
  152.4 4.9 %shard_map.146 = (bf16[1,128,2048]{2,1,0:T(8,128)(2,1)}, bf16[1,128,2048]{2,1,0:T(8,128)(2,1)}, bf16[1,128,2048]{2,1,0:T(8,128)(2,1)}, bf16[1,128,2048]{2,1,0:T(...) custom-call(bf16[128,2048]{1,0:T(8,128)(2,1)} %get-tuple-element.11.q, ...), custom_call_target="tpu_custom_call" | custom-call | tf_op jit(solution)/shard_map/pallas_call | solution.py:592

commit v2 on v1

--- a/solution.py
+++ b/solution.py
@@ -84,12 +84,6 @@
         pl.semaphore_signal(barrier, inc=1, device_id=other, device_id_type=MESH)
     pl.semaphore_wait(barrier, NS - 1 + 4)
 
-    tabt[0, core] = table[...].T
-    table_over = remote(tabt.at[0, core], tabt.at[1, core], t_send.at[0], t_recv.at[0], over_x)
-    table_over.start()
-    table_sib = remote(tabt.at[0, core], tabt.at[0, core], t_send.at[1], t_recv.at[1], sib)
-    table_sib.start()
-
     mine = pl.ds(pl.multiple_of(me * TB, TB), TB)
     sources = (sq, sk, up, sv, cq)
 
@@ -114,9 +108,18 @@
         pltpu.make_async_copy(
             sources[a].at[:, pl.ds(pl.multiple_of(me * HD, HD), HD)], abuf.at[a, mine], loc.at[a]
         ).start()
+    send_in(0, 0)
+
+    tabt[0, core] = table[...].T
+    table_over = remote(tabt.at[0, core], tabt.at[1, core], t_send.at[0], t_recv.at[0], over_x)
+    table_over.start()
+    table_sib = remote(tabt.at[0, core], tabt.at[0, core], t_send.at[1], t_recv.at[1], sib)
+    table_sib.start()
+
     for dx in range(2):
         for a in EARLY:
-            send_in(a, dx)
+            if (a, dx) != (0, 0):
+                send_in(a, dx)
     w_in = [pltpu.make_async_copy(w, wbuf.at[i], loc.at[5 + i]) for i, w in enumerate((kw, vw))]
     for copy in w_in:
         copy.start()
@@ -154,11 +157,6 @@
     table_over.wait_recv()
     table_on = remote(tabt.at[1, core], tabt.at[1, core], t_send.at[2], t_recv.at[2], sib)
     table_on.start()
-
-    for i, copy in enumerate(w_in):
-        copy.wait()
-        for j in range(NS):
-            wt[i * HD : (i + 1) * HD, j * CW : (j + 1) * CW] = wbuf[i, j * CW : (j + 1) * CW, :].T
 
     low, high = pl.ds(0, HC), pl.ds(HC, HC)
     table_on.wait_recv()
@@ -316,17 +314,20 @@
 
     gather_start()
     later("start")
+    for i, copy in enumerate(w_in):
+        copy.wait()
+        for j in range(NS):
+            wt[i * HD : (i + 1) * HD, j * CW : (j + 1) * CW] = wbuf[i, j * CW : (j + 1) * CW, :].T
+    gather_step(0)
+    later("step0")
     arrived(0)
     arrived(1)
     for k in range(T // KC):
         kt[:, k * KC : (k + 1) * KC] = abuf[1, k * KC : (k + 1) * KC, :].T
-    lax.fori_loop(0, 2, first, 0)
-    gather_step(0)
-    later("step0")
-    lax.fori_loop(2, 4, first, 0)
+    lax.fori_loop(0, 3, first, 0)
     gather_step(1)
     later("step1")
-    lax.fori_loop(4, 6, first, 0)
+    lax.fori_loop(3, 6, first, 0)
     gather_step(2)
     later("step2")
     lax.fori_loop(6, 8, first, 0)

time: 158 us -> 157 us (level)
  no operation moved by 1% of the time
where the time goes in v2:
time: 157 us
  Pallas kernels  156 us (99%)
    pallas_call x1, Pallas kernels, on_device(): pl.pallas_call(kernel, out_shape=[token_grad] * 4 + [weight_grads], in_sp...  151 us
    pallas_call x1, Pallas kernels, on_device(): pl.pallas_call(leave_kernel, grid=(cuts,), out_shape=[jax.ShapeDtypeStruc...  4.89 us

profile of v2, /device:TPU:1, one launch (start us, length us, event | category | flops | bytes accessed | tf_op | source)
XLA Modules:
  0.0 156.6 jit_solution(17447917149660122995)
XLA Ops:
  0.6 151.0 %shard_map.145 = (bf16[128,2048]{1,0:T(8,128)(2,1)}, bf16[128,2048]{1,0:T(8,128)(2,1)}, bf16[128,2048]{1,0:T(8,128)(2,1)}, bf16[128,2048]{1,0:T(8,128)(2,1)}, bf16[2,4,2,256,256]{4,3,2,1,0:T(8,128)(2,1)}) custom-call(bf16[128,2048]{1,0:T(8,128)(2,1)} %bitcast.7, bf16[128,2048]{1,0:T(8,128)(2,1)} %bitcast.8, bf16[128,2048]{1,0:T(8,128)(2,1)} %bitcast.9, ...), custom_call_target="tpu_custom_call" | custom-call | tf_op jit(solution)/shard_map/pallas_call | solution.py:537
  151.7 4.9 %shard_map.146 = (bf16[1,128,2048]{2,1,0:T(8,128)(2,1)}, bf16[1,128,2048]{2,1,0:T(8,128)(2,1)}, bf16[1,128,2048]{2,1,0:T(8,128)(2,1)}, bf16[1,128,2048]{2,1,0:T(...) custom-call(bf16[128,2048]{1,0:T(8,128)(2,1)} %get-tuple-element.11.q, ...), custom_call_target="tpu_custom_call" | custom-call | tf_op jit(solution)/shard_map/pallas_call | solution.py:593
